TPU v7x, 32 devices: a whole 2x2x4 slice. The times are simulated.
32 devices in a mesh: parts: 1, row: 8 (over z, y), col: 1, depth: 4 (over x, core).
Axes of the slice: x: 2, y: 2, z: 4, core: 2. Of those that a mesh axis runs over, the one named last changes fastest.
Arguments:
- activations: bfloat16 [4, 256, 8192], P(('parts', 'depth'), 'row', 'col'), may hold values from -6 to 6
- hidden_grads: bfloat16 [4, 256, 16384], P(('parts', 'depth'), 'col', 'row'), may hold values from -0.1875 to 0.1875
Outputs:
- weight_grad: bfloat16 [8192, 16384], P(('parts', 'col', 'depth'), 'row')
All inputs are finite; a program needn't handle non-finite values.
Results may differ from a plain program's by a relative error of at most 0.013.
Values may be sent and summed in bfloat16 or wider, within the bound.
A program may use at most 128 MiB of HBM per device.

v0:
```python
import jax
import jax.numpy as jnp
from jax import lax
from jax.sharding import PartitionSpec as P


def local(activations, hidden_grads):
    swapped = lax.all_to_all(activations, "depth", split_axis=2, concat_axis=0, tiled=True)
    acts = lax.all_gather(swapped, "row", axis=1, tiled=True)
    grads = lax.all_gather(hidden_grads, "depth", axis=0, tiled=True)
    grads = lax.all_gather(grads, "col", axis=1, tiled=True)
    total = lax.dot_general(
        acts, grads, (((0, 1), (0, 1)), ((), ())), preferred_element_type=jnp.float32
    )
    return total.astype(jnp.bfloat16)


def solution(mesh):
    in_specs = (P(("parts", "depth"), "row", "col"), P(("parts", "depth"), "col", "row"))
    out_specs = P(("parts", "col", "depth"), "row")
    return jax.shard_map(local, mesh=mesh, in_specs=in_specs, out_specs=out_specs, check_vma=False)
```

profile of v0, /device:TPU:0, one launch (start us, length us, event | category | flops | bytes accessed | tf_op | source)
XLA Modules:
  0.0 217.2 jit_solution(3695399159835913625)
XLA Ops:
  6.5 0.0 all-gather.6.cloned.1.call-start
  6.5 8.6 %copy.7 = bf16[1,32,8192]{1,0,2:T(2,128)(2,1)} copy(bf16[1,32,8192]{2,1,0:T(8,128)(2,1)} %param.2) | data formatting | bytes 1048576 | tf_op args[0]
  15.1 0.5 broadcast
  15.6 45.2 %reduce = bf16[8192,32]{1,0:T(8,128)(2,1)S(1)} reduce(bf16[8192,1,32]{2,1,0:T(2,128)(2,1)} %bitcast.11, bf16[]{:T(256)} %broadcast), dimensions={1}, to_apply=%bitcast.8.reduce_sub_computation | reduce | bytes 1048578
  60.8 2.2 reshape.2
  63.0 12.9 %all_to_all.18 = bf16[4,2,32768]{2,1,0:T(2,128)(2,1)S(1)} all-to-all(bf16[4,2,32768]{2,1,0:T(2,128)(2,1)S(1)} %reshape.2), channel_id=1, replica_groups=mesh['parts'=1,'row'=8,'col'=1,'depth'=4] {'depth'}, dimensions={0} | all-to-all | bytes 1048576 | tf_op jit(solution)/shard_map/all_to_all | solution.py:8
  75.9 3.3 %reshape.3 = bf16[8192,1,32]{2,1,0:T(2,128)(2,1)} reshape(bf16[4,2,32768]{2,1,0:T(2,128)(2,1)S(1)} %all_to_all.18) | data formatting | bytes 1048576
  79.1 8.0 %copy.8 = bf16[1,32,8192]{2,1,0:T(8,128)(2,1)S(1)} copy(bf16[1,32,8192]{1,0,2:T(2,128)(2,1)} %bitcast.12) | data formatting | bytes 1048576 | tf_op jit(solution)/shard_map/all_to_all | solution.py:8
  87.1 1.2 all_to_all.14
  88.3 0.0 all-gather.6.cloned.1.call-update
  88.3 0.2 all-gather.4.cloned.1.call-start
  88.5 0.5 all-gather.4.cloned.1.call-update
  89.0 73.1 %all-gather.6.cloned.1.call-done = bf16[4,1,256,2048]{3,0,1,2:T(4,128)(2,1)} async-done(((bf16[4,1,32,2048]{3,0,1,2:T(4,128)(2,1)}), bf16[4,1,256,2048]{3,0,1,2:T(4,128)(2,1)}) %all-gather.6.cloned.1.call-update) | async-done | bytes 4194320 | tf_op jit(solution)/shard_map/all_gather | solution.py:9
  162.2 7.6 %copy.10 = bf16[4,1,256,2048]{2,3,0,1:T(8,128)(2,1)} copy(bf16[4,1,256,2048]{3,0,1,2:T(4,128)(2,1)} %all-gather.6.cloned.1.call-done) | data formatting | bytes 8388608 | tf_op jit(solution)/shard_map/all_gather | solution.py:9
  169.7 26.8 %all-gather.4.cloned.1.call-done = bf16[4,256,2048]{2,1,0:T(8,128)(2,1)} async-done(((bf16[1,256,2048]{2,1,0:T(8,128)(2,1)}), bf16[4,256,2048]{2,1,0:T(8,128)(2,1)}) %all-gather.4.cloned.1.call-update) | async-done | bytes 4194320 | tf_op jit(solution)/shard_map/all_gather | solution.py:10
  196.5 13.9 %bitcast_convert_fusion = bf16[2048,2048]{1,0:T(8,128)(2,1)} fusion(bf16[4,256,2048]{2,1,0:T(8,128)(2,1)} %all-gather.4.cloned.1.call-done, bf16[4,1,256,2048]{2,3,0,1:T(8,128)(2,1)} %copy.10), kind=kOutput, calls=%fused_computation | convolution fusion | flops 8594128896 | bytes 16777216 | tf_op jit(solution)/shard_map/dot_general | solution.py:12
Async XLA Ops:
  6.5 155.6 %all-gather.6.cloned.1.call-start = ((), (), s32[]{:S(2)}) async-start(), calls=%async_computation.2 | async-start | bytes 4718592 | tf_op jit(solution)/shard_map/all_gather | solution.py:9
  88.3 108.2 %all-gather.4.cloned.1.call-start = ((), (), s32[]{:S(2)}) async-start(), calls=%async_computation.1 | async-start | bytes 5242880 | tf_op jit(solution)/shard_map/all_gather | solution.py:10
Sparse Core Ops, SparseCore 0:
  88.4 73.7 all-gather.5
  163.7 32.7 all-gather.3
where the time goes:
time: 218 us; the launch traced here: 217 us
  waiting for transfers between devices  100 us (46%)
  other arithmetic  45.2 us (21%)
  local copies, waits for them, and re-layouts  31.2 us (14%)
  matrix products  13.9 us (6%)
  between operations  13.4 us (6%)
  blocking collectives  12.9 us (6%)
    all_gather x1, waiting for transfers between devices, local(): acts = lax.all_gather(swapped, 'row', axis=1, tiled=True)  73.1 us
    unnamed x1, other arithmetic  45.2 us
    all_gather x1, waiting for transfers between devices, local(): grads = lax.all_gather(hidden_grads, 'depth', axis=0, tiled=True)  26.8 us
    unnamed x4, local copies, waits for them, and re-layouts  14.5 us
    dot_general x1, matrix products, local(): lax.dot_general(acts, grads, (((0, 1), (0, 1)), ((), ())), preferred_elem...  13.9 us
    all_to_all x1, blocking collectives, local(): lax.all_to_all(activations, 'depth', split_axis=2, concat_axis=0, tiled=T...  12.9 us
    all_to_all x2, local copies, waits for them, and re-layouts, local(): lax.all_to_all(activations, 'depth', split_axis=2, concat_axis=0, tiled=T...  9.14 us
    all_gather x1, local copies, waits for them, and re-layouts, local(): acts = lax.all_gather(swapped, 'row', axis=1, tiled=True)  7.56 us
  transfers between devices with their start and end apart: 2, of which 2 were waited for; matrix products, arithmetic and copies ran while one was open for 3% of the time, Pallas kernels for 0%

commit v1 on v0

--- a/solution.py
+++ b/solution.py
@@ -5,7 +5,15 @@
 
 
 def local(activations, hidden_grads):
-    swapped = lax.all_to_all(activations, "depth", split_axis=2, concat_axis=0, tiled=True)
+    swapped = jnp.concatenate(
+        lax.all_to_all(
+            jnp.stack(jnp.split(activations, lax.axis_size("depth"), 2), axis=0),
+            "depth",
+            split_axis=0,
+            concat_axis=0,
+        ),
+        0,
+    )
     acts = lax.all_gather(swapped, "row", axis=1, tiled=True)
     grads = lax.all_gather(hidden_grads, "depth", axis=0, tiled=True)
     grads = lax.all_gather(grads, "col", axis=1, tiled=True)

time: 218 us -> 151 us (0.69)
  other arithmetic: 45.2 us -> 0.07 us
  local copies, waits for them, and re-layouts: 31.2 us -> 9.95 us
    unnamed x1 -> x0, other arithmetic: 45.2 us -> none
    unnamed x4 -> x0, local copies, waits for them, and re-layouts: 14.5 us -> none
    all_to_all x2 -> x1, local copies, waits for them, and re-layouts: 9.14 us -> 1.2 us  [local(): lax.all_to_all(jnp.stack(jnp.split(activations, lax.axis_size('depth'), 2...]
  transfers between devices with their start and end apart: 2 -> 2, of which waited for: 2 -> 2; matrix products, arithmetic and copies ran while one was open for 3% -> 5% of each run, Pallas kernels for 0% -> 0%
where the time goes in v1:
time: 151 us
  waiting for transfers between devices  101 us (67%)
  matrix products  13.9 us (9%)
  between operations  13.4 us (9%)
  blocking collectives  12.9 us (9%)
  local copies, waits for them, and re-layouts  9.95 us (7%)
    all_gather x1, waiting for transfers between devices, local(): acts = lax.all_gather(swapped, 'row', axis=1, tiled=True)  73.1 us
    all_gather x1, waiting for transfers between devices, local(): grads = lax.all_gather(hidden_grads, 'depth', axis=0, tiled=True)  26.7 us
    dot_general x1, matrix products, local(): lax.dot_general(acts, grads, (((0, 1), (0, 1)), ((), ())), preferred_elem...  13.9 us
    all_to_all x1, blocking collectives, local(): lax.all_to_all(jnp.stack(jnp.split(activations, lax.axis_size('depth'), 2...  12.9 us
    all_gather x1, local copies, waits for them, and re-layouts, local(): acts = lax.all_gather(swapped, 'row', axis=1, tiled=True)  7.62 us
  transfers between devices with their start and end apart: 2, of which 2 were waited for; matrix products, arithmetic and copies ran while one was open for 5% of the time, Pallas kernels for 0%

profile of v1, /device:TPU:0, one launch (start us, length us, event | category | flops | bytes accessed | tf_op | source)
XLA Modules:
  0.0 150.8 jit_solution(44746954799087093)
XLA Ops:
  6.5 0.0 all-gather.6.cloned.1.call-start
  6.5 1.1 slice_bitcast_fusion.3
  7.7 0.1 pad_maximum_fusion
  7.7 12.9 %all_to_all.5 = bf16[4,1,32,2048]{3,2,1,0:T(8,128)(2,1)S(1)} all-to-all(bf16[4,1,32,2048]{3,2,1,0:T(8,128)(2,1)S(1)} %pad_maximum_fusion), channel_id=1, replica_groups=mesh['parts'=1,'row'=8,'col'=1,'depth'=4] {'depth'}, dimensions={0} | all-to-all | bytes 1048576 | tf_op jit(solution)/shard_map/all_to_all | solution.py:9
  20.6 1.2 copy.7
  21.8 0.0 all-gather.6.cloned.1.call-update
  21.8 0.0 all-gather.4.cloned.1.call-start
  21.9 0.7 all-gather.4.cloned.1.call-update
  22.6 73.1 %all-gather.6.cloned.1.call-done = bf16[4,1,256,2048]{3,0,1,2:T(4,128)(2,1)} async-done(((bf16[4,1,32,2048]{3,0,1,2:T(4,128)(2,1)}), bf16[4,1,256,2048]{3,0,1,2:T(4,128)(2,1)}) %all-gather.6.cloned.1.call-update) | async-done | bytes 4194320 | tf_op jit(solution)/shard_map/all_gather | solution.py:17
  95.7 7.6 %copy.8 = bf16[4,1,256,2048]{2,3,0,1:T(8,128)(2,1)} copy(bf16[4,1,256,2048]{3,0,1,2:T(4,128)(2,1)} %all-gather.6.cloned.1.call-done) | data formatting | bytes 8388608 | tf_op jit(solution)/shard_map/all_gather | solution.py:17
  103.3 26.7 %all-gather.4.cloned.1.call-done = bf16[4,256,2048]{2,1,0:T(8,128)(2,1)} async-done(((bf16[1,256,2048]{2,1,0:T(8,128)(2,1)}), bf16[4,256,2048]{2,1,0:T(8,128)(2,1)}) %all-gather.4.cloned.1.call-update) | async-done | bytes 4194320 | tf_op jit(solution)/shard_map/all_gather | solution.py:18
  130.0 13.9 %bitcast_convert_fusion = bf16[2048,2048]{1,0:T(8,128)(2,1)} fusion(bf16[4,256,2048]{2,1,0:T(8,128)(2,1)} %all-gather.4.cloned.1.call-done, bf16[4,1,256,2048]{2,3,0,1:T(8,128)(2,1)} %copy.8), kind=kOutput, calls=%fused_computation | convolution fusion | flops 8594128896 | bytes 16777216 | tf_op jit(solution)/shard_map/dot_general | solution.py:20
Async XLA Ops:
  6.5 89.2 %all-gather.6.cloned.1.call-start = ((), (), s32[]{:S(2)}) async-start(), calls=%async_computation.2 | async-start | bytes 4718592 | tf_op jit(solution)/shard_map/all_gather | solution.py:17
  21.8 108.2 %all-gather.4.cloned.1.call-start = ((), (), s32[]{:S(2)}) async-start(), calls=%async_computation.1 | async-start | bytes 5242880 | tf_op jit(solution)/shard_map/all_gather | solution.py:18
Sparse Core Ops, SparseCore 0:
  21.9 73.7 all-gather.5
  97.3 32.7 all-gather.3
